TPU v7x, 256 devices: a whole 4x4x8 slice. The times are simulated.
256 devices in a mesh: req: 32 (over y, x, core), tp: 8 (over z).
Axes of the slice: x: 4, y: 4, z: 8, core: 2. Of those that a mesh axis runs over, the one named last changes fastest.
Arguments:
- queries: bfloat16 [2048, 8192], P('req', 'tp'), may hold values from -120 to 120
- key_cache: bfloat16 [2048, 8, 64, 128], P('req', 'tp'), may hold values from -4.1 to 4.1
- value_cache: bfloat16 [2048, 8, 64, 128], P('req', 'tp'), may hold values from -6 to 6
- new_key: bfloat16 [2048, 1024], P('req', 'tp'), may hold values from -6 to 6
- new_value: bfloat16 [2048, 1024], P('req', 'tp'), may hold values from -6 to 6
- cache_length: int32 [2048], P('req'), may hold values from 1 to 64, 65536 in all
- row_adapter: int32 [2048, 1], P('req'), may hold values from 0 to 63; in each aligned block of 64 rows (0 to 63, 64 to 127, ...) at most 2 rows name the same one
- adapter_home: int32 [64], replicated, may hold values from 0 to 63, each once
- down_pool: bfloat16 [64, 8192, 16], P('req', 'tp'), may hold values from -0.0625 to 0.0625
- up_pool: bfloat16 [64, 16, 4096], P('req', None, 'tp'), may hold values from -1.5 to 1.5
- out_weight: bfloat16 [8192, 4096], P('tp'), may hold values from -0.0625 to 0.0625
Outputs:
- mixed: bfloat16 [2048, 4096], P('req', 'tp')
Inputs may be any that keep to these rules, and one draw needn't show every extreme that they name: `row_adapter`: among the 64 rows of one group no adapter is named by more than 2 rows, and some group has 2 rows on one adapter. `adapter_home`: a permutation; slot s is held by index s // 2 of req.
All inputs are finite; a program needn't handle non-finite values. No bound on the sum of `cache_length` on one device may be relied on, other than what follows from the above.
Results may differ from a plain program's by a relative error of at most 0.015.
Values may be sent and summed in bfloat16 or wider, within the bound.
A program may use at most 64 MiB of HBM per device.

v0:
```python
import jax
import jax.numpy as jnp
from jax import lax
from jax.sharding import PartitionSpec as P

HEAD_DIM = 128
GROUP = 8


def attend(queries, key_cache, value_cache, new_key, new_value, cache_length):
    count = queries.shape[0]
    kv_local = key_cache.shape[1]
    positions = key_cache.shape[2]
    scale = 1.0 / HEAD_DIM**0.5
    query = queries.reshape(count, kv_local, GROUP, HEAD_DIM)
    fresh_key = new_key.reshape(count, kv_local, HEAD_DIM)
    fresh_value = new_value.reshape(count, kv_local, HEAD_DIM)
    scores = (
        jnp.einsum("rkgd,rkld->rkgl", query, key_cache, preferred_element_type=jnp.float32) * scale
    )
    fresh = (
        jnp.einsum("rkgd,rkd->rkg", query, fresh_key, preferred_element_type=jnp.float32) * scale
    )
    valid = jnp.arange(positions, dtype=jnp.int32)[None, :] < cache_length[:, None]
    valid = valid[:, None, None, :]
    scores = jnp.where(valid, scores, -1e30)
    top = jnp.maximum(jnp.max(scores, axis=3), fresh)
    expo = jnp.where(valid, jnp.exp(scores - top[..., None]), 0.0)
    fresh_expo = jnp.exp(fresh - top)
    total = jnp.sum(expo, axis=3) + fresh_expo
    weights = (expo / total[..., None]).astype(jnp.bfloat16)
    fresh_weight = (fresh_expo / total).astype(jnp.bfloat16)
    mixed = jnp.einsum("rkgl,rkld->rkgd", weights, value_cache, preferred_element_type=jnp.float32)
    mixed = (
        mixed
        + fresh_weight.astype(jnp.float32)[..., None]
        * fresh_value.astype(jnp.float32)[:, :, None, :]
    )
    return mixed.reshape(count, kv_local * GROUP * HEAD_DIM).astype(jnp.bfloat16)


def per_device(
    queries,
    key_cache,
    value_cache,
    new_key,
    new_value,
    cache_length,
    row_adapter,
    adapter_home,
    down_pool,
    up_pool,
    out_weight,
):
    attended = attend(queries, key_cache, value_cache, new_key, new_value, cache_length)
    slot_dev = down_pool.shape[0]
    groups = lax.axis_size("req")
    total_slots = slot_dev * groups
    slot_ids = jnp.arange(total_slots, dtype=jnp.int32)
    named = row_adapter[:, 0]
    slot = jnp.sum(jnp.where(named[:, None] == slot_ids[None, :], adapter_home[None, :], 0), axis=1)
    base = jnp.dot(attended, out_weight, preferred_element_type=jnp.float32)
    piece = lax.all_gather(down_pool, "req", axis=0, tiled=True)
    number = piece.shape[0]
    product = jnp.einsum("rh,khq->rkq", attended, piece, preferred_element_type=jnp.float32)
    pick = (slot[:, None] == jnp.arange(number, dtype=jnp.int32)[None, :]).astype(jnp.float32)
    partial_low = jnp.sum(pick[:, :, None] * product, axis=1)
    low = lax.psum(partial_low, "tp").astype(jnp.bfloat16)
    piece = lax.all_gather(up_pool, "req", axis=0, tiled=True)
    number = piece.shape[0]
    product = jnp.einsum("rq,kqd->rkd", low, piece, preferred_element_type=jnp.float32)
    pick = (slot[:, None] == jnp.arange(number, dtype=jnp.int32)[None, :]).astype(jnp.float32)
    delta = jnp.sum(pick[:, :, None] * product, axis=1)
    delta = delta.astype(jnp.bfloat16).astype(jnp.float32)
    share = lax.psum_scatter(base, "tp", scatter_dimension=1, tiled=True)
    return (share + delta).astype(jnp.bfloat16)


def solution(mesh):
    return jax.shard_map(
        per_device,
        mesh=mesh,
        in_specs=(
            P("req", "tp"),
            P("req", "tp", None, None),
            P("req", "tp", None, None),
            P("req", "tp"),
            P("req", "tp"),
            P("req"),
            P("req", None),
            P(),
            P("req", "tp", None),
            P("req", None, "tp"),
            P("tp", None),
        ),
        out_specs=P("req", "tp"),
        check_vma=False,
    )
```

profile of v0, /device:TPU:1, one launch (start us, length us, event | category | flops | bytes accessed | tf_op | source)
XLA Modules:
  0.0 125.1 jit_solution(9273895316214713143)
XLA Ops:
  7.4 0.0 copy-start
  7.4 0.0 all-gather.3.cloned.1.call-start
  7.4 0.7 all-gather.3.cloned.1.call-update
  8.1 0.0 all-gather.5.cloned.1.call-start
  8.1 0.7 all-gather.5.cloned.1.call-update
  8.8 0.0 reduce-scatter.2.cloned.1.call-start
  8.9 0.9 copy.25
  9.8 0.7 convert_element_type.45
  10.5 0.7 iota_compare_fusion.2
  11.3 0.9 fusion.20
  12.2 2.0 %fusion.28 = (f32[64,8]{1,0:T(8,128)S(1)}, f32[64,8,64]{2,1,0:T(8,128)S(1)}) fusion(bf16[64,8,128]{2,1,0:T(8,128)(2,1)S(1)} %bitcast.28, bf16[64,1,64,128]{3,2,1,0:T(8,128)(2,1)} %param.12, pred[64,64]{1,0:T(8,128)(4,1)S(1)} %iota_compare_fusion.2), kind=kOutput, calls=%fused_computation.37 | convolution fusion | flops 8486400 | bytes 1316864 | tf_op jit(solution)/shard_map/rkgd,rkld->rkgl/dot_general | solution.py:19
  14.2 0.2 fusion.12
  14.4 0.0 copy-done
  14.4 0.5 fusion.9
  14.9 0.0 copy-start.1
  14.9 0.0 copy-start.2
  14.9 5.9 %fusion.13 = f32[64,4096]{1,0:T(8,128)} fusion(bf16[1024,4096]{1,0:T(8,128)(2,1)} %param.21, bf16[8,8,8,128]{3,2,1,0:T(8,128)(2,1)S(1)} %bitcast.26), kind=kOutput, calls=%fused_computation.14 | convolution fusion | flops 536870912 | bytes 9568256 | tf_op jit(solution)/shard_map/dot_general | solution.py:62
  20.9 0.0 reduce-scatter.2.cloned.1.call-update
  20.9 0.1 reshape.112
  21.0 0.0 copy-done.1
  21.0 0.0 copy-done.2
  21.0 0.2 select_reduce_fusion
  21.2 42.7 %all-gather.3.cloned.1.call-done = bf16[64,1024,16]{1,2,0:T(8,128)(2,1)} async-done(((bf16[2,1024,16]{1,2,0:T(8,128)(2,1)}), bf16[64,1024,16]{1,2,0:T(8,128)(2,1)}) %all-gather.3.cloned.1.call-update) | async-done | bytes 2097168 | tf_op jit(solution)/shard_map/all_gather | solution.py:63
  63.9 3.9 %fusion.5 = f32[64,16]{0,1:T(8,128)S(1)} fusion(bf16[64,1024,1]{1,0,2:T(8,128)(2,1)S(1)} %reshape.112, bf16[64,1024,16]{1,2,0:T(8,128)(2,1)} %all-gather.3.cloned.1.call-done, f32[64,64]{0,1:T(8,128)S(1)} %fusion.22), kind=kOutput, calls=%fused_computation.4 | convolution fusion | flops 134347776 | bytes 2248704 | tf_op jit(solution)/shard_map/rh,khq->rkq/dot_general | solution.py:65
  67.8 14.0 %psum.7 = bf16[64,16]{0,1:T(8,128)(2,1)S(1)} all-reduce(f32[64,16]{0,1:T(8,128)S(1)} %fusion.5), channel_id=1, replica_groups=mesh['req'=32,'tp'=8] {'tp'}, use_global_device_ids=true, to_apply=%region_5.6 | all-reduce | flops 1024 | bytes 6144 | tf_op jit(solution)/shard_map/psum | solution.py:68
  81.8 31.8 %all-gather.5.cloned.1.call-done = bf16[64,16,512]{2,1,0:T(8,128)(2,1)} async-done(((bf16[2,16,512]{2,1,0:T(8,128)(2,1)}), bf16[64,16,512]{2,1,0:T(8,128)(2,1)}) %all-gather.5.cloned.1.call-update) | async-done | bytes 1048592 | tf_op jit(solution)/shard_map/all_gather | solution.py:69
  113.5 2.5 %multiply_reduce_fusion = bf16[64,512]{1,0:T(8,128)(2,1)S(1)} fusion(f32[64,64]{0,1:T(8,128)S(1)} %fusion.22, bf16[64,16,512]{2,1,0:T(8,128)(2,1)} %all-gather.5.cloned.1.call-done, bf16[64,16]{0,1:T(8,128)(2,1)S(1)} %psum.7), kind=kOutput, calls=%fused_computation | convolution fusion | flops 71270400 | bytes 1132544 | tf_op jit(solution)/shard_map/rq,kqd->rkd/dot_general | solution.py:71
  116.0 0.0 reduce-scatter.2.cloned.1.call-done
  116.1 1.5 %add_convert_fusion = bf16[64,512]{1,0:T(8,128)(2,1)} fusion(f32[64,512]{1,0:T(8,128)} %reduce-scatter.2.cloned.1.call-done, bf16[64,512]{1,0:T(8,128)(2,1)S(1)} %multiply_reduce_fusion), kind=kLoop, calls=%fused_computation.17 | loop fusion | flops 98304 | bytes 262144 | tf_op jit(solution)/shard_map/convert_element_type | solution.py:76
  (3 shorter events, 0.0 us)
Async XLA Ops:
  7.4 7.1 %copy-start = (bf16[64,1,64,128]{3,2,1,0:T(8,128)(2,1)S(1)}, bf16[64,1,64,128]{3,2,1,0:T(8,128)(2,1)}, u32[]{:S(2)}) copy-start(bf16[64,1,64,128]{3,2,1,0:T(8,128)(2,1)} %param.13) | copy-start | bytes 3145732
  7.4 56.5 %all-gather.3.cloned.1.call-start = ((), (), s32[]{:S(2)}) async-start(), calls=%async_computation.2 | async-start | bytes 2162688 | tf_op jit(solution)/shard_map/all_gather | solution.py:63
  8.1 105.4 %all-gather.5.cloned.1.call-start = ((), (), s32[]{:S(2)}) async-start(), calls=%async_computation.3 | async-start | bytes 1081344 | tf_op jit(solution)/shard_map/all_gather | solution.py:69
  8.8 107.2 %reduce-scatter.2.cloned.1.call-start = ((), (), s32[]{:S(2)}) async-start(), calls=%async_computation.1 | async-start | bytes 1179648 | tf_op jit(solution)/shard_map/reduce_scatter | solution.py:75
  14.9 6.1 %copy-start.1 = (s32[64]{0:T(128)S(1)}, s32[64]{0:T(128)}, u32[]{:S(2)}) copy-start(s32[64]{0:T(128)} %param.18) | copy-start | bytes 772
  14.9 6.1 %copy-start.2 = (s32[64,1]{0,1:T(1,128)S(1)}, s32[64,1]{0,1:T(1,128)}, u32[]{:S(2)}) copy-start(s32[64,1]{0,1:T(1,128)} %param.17) | copy-start | bytes 772
Sparse Core Ops, SparseCore 0:
  10.7 53.0 all-gather.2
  66.4 47.0 all-gather.4
Sparse Core Ops, SparseCore 1:
  21.0 37.3 reduce-scatter.1
where the time goes:
time: 125 us
  waiting for transfers between devices  75.9 us (61%)
  matrix products  15.7 us (13%)
  between operations  15 us (12%)
  blocking collectives  14 us (11%)
  other arithmetic  3.44 us (3%)
    all_gather x1, waiting for transfers between devices, per_device(): piece = lax.all_gather(down_pool, 'req', axis=0, tiled=True)  42.7 us
    all_gather x1, waiting for transfers between devices, per_device(): piece = lax.all_gather(up_pool, 'req', axis=0, tiled=True)  31.8 us
    psum x1, blocking collectives, per_device(): low = lax.psum(partial_low, 'tp').astype(jnp.bfloat16)  14 us
    dot_general x1, matrix products, per_device(): base = jnp.dot(attended, out_weight, preferred_element_type=jnp.float32)  5.95 us
    dot_general x1, matrix products, per_device(): jnp.einsum('rh,khq->rkq', attended, piece, preferred_element_type=jnp.flo...  3.94 us
    dot_general x1, matrix products, per_device(): jnp.einsum('rq,kqd->rkd', low, piece, preferred_element_type=jnp.float32)  2.5 us
  transfers between devices with their start and end apart: 3, of which 2 were waited for; matrix products, arithmetic and copies ran while one was open for 15% of the time, Pallas kernels for 0%

commit v1 on v0

v1 whole, which is shorter than its diff:
```python
import jax
import jax.numpy as jnp
from jax import lax
from jax.experimental import pallas as pl
from jax.experimental.pallas import tpu as pltpu
from jax.sharding import PartitionSpec as P

MESH = pl.DeviceIdType.MESH
HEAD_DIM = 128
GROUP = 8
ROWS = 64
CACHE = 64
RANK = 16
NEG = -1e30
ORDER = (4, 3, -3, 2, -2, 1, -1, 0)


def kernel(
    q_hbm, k_hbm, v_hbm, nk_hbm, nv_hbm, len_hbm, ad_hbm, home_hbm, down_hbm, up_hbm, w_hbm,
    out_ref,
    q, kk, vv, nk, nv, lens, ad, home, gath, w, att, part, low_own, low_all, rs_src, rs_dst,
    in_sem, kv_sem, w_sem, ag_send, ag_recv, low_send, low_recv, rs_send, rs_recv,
):
    req, z = lax.axis_index("req"), lax.axis_index("tp")
    core = req % 2
    x = (req // 2) % 4
    y = req // 8

    a_me = jnp.where(core == 0, x, y)
    b_me = jnp.where(core == 0, y, x)

    def at(yy, xx, cc):
        return ((yy * 4 + xx) * 2 + cc, z)

    def peer_a(d):
        return at((y + core * d) % 4, (x + (1 - core) * d) % 4, core)

    def peer_b(d):
        return at((y + (1 - core) * d) % 4, (x + core * d) % 4, core)

    sibling = at(y, x, 1 - core)

    def bundle(b):
        return (core * 4 + b % 4) * 128

    own_row = bundle(b_me) + a_me * 32

    loads = [
        (len_hbm, lens), (ad_hbm, ad), (home_hbm, home), (q_hbm, q), (nk_hbm, nk), (nv_hbm, nv),
        (down_hbm.at[:, pl.ds(0, 512)], gath.at[0, pl.ds(pl.multiple_of(own_row, 32), 32)]),
        (down_hbm.at[:, pl.ds(512, 512)], gath.at[1, pl.ds(pl.multiple_of(own_row, 32), 32)]),
        (up_hbm, gath.at[2, pl.ds(pl.multiple_of(own_row, 32), 32)]),
    ]
    loads = [pltpu.make_async_copy(s, d, in_sem.at[i]) for i, (s, d) in enumerate(loads)]
    for i in (6, 7, 8, 3, 0, 4, 5, 1, 2):
        loads[i].start()
    kv = []
    for i in range(4):
        rows = pl.ds(1024 * i, 1024)
        kv.append(pltpu.make_async_copy(k_hbm.at[rows], kk.at[rows], kv_sem.at[0, i]))
        kv.append(pltpu.make_async_copy(v_hbm.at[rows], vv.at[rows], kv_sem.at[1, i]))
    for c in kv:
        c.start()
    ws = []
    for n, o in enumerate(ORDER):
        col = pl.multiple_of(((z + o + 8) % 8) * 512, 512)
        ws.append(pltpu.make_async_copy(w_hbm.at[:, pl.ds(col, 512)], w.at[n], w_sem.at[n]))
        ws[-1].start()

    barrier = pltpu.get_barrier_semaphore()
    peers = [peer_a(1), peer_a(3), peer_a(2), peer_b(1), peer_b(3), sibling]
    peers += [(req, (z + d) % 8) for d in range(1, 8)]
    for p in peers:
        pl.semaphore_signal(barrier, inc=1, device_id=p, device_id_type=MESH)
    pl.semaphore_wait(barrier, len(peers))

    started = []

    def ag_copy(chunk, slot, row, rows, device):
        ref = gath.at[chunk, pl.ds(pl.multiple_of(row, 32), rows)]
        copy = pltpu.make_async_remote_copy(
            src_ref=ref, dst_ref=ref, send_sem=ag_send.at[chunk, slot], recv_sem=ag_recv.at[chunk, slot],
            device_id=device, device_id_type=MESH,
        )
        copy.start()
        started.append(copy)
        return copy

    ag = [dict() for _ in range(3)]

    def ag_first(chunk):
        d = ag[chunk]
        d["a"] = [ag_copy(chunk, i, own_row, 32, peer_a(s)) for i, s in enumerate((1, 3, 2))]

    def ag_second(chunk):
        d = ag[chunk]
        for c in d["a"]:
            c.wait_recv()
        row = bundle(b_me)
        d["up"] = ag_copy(chunk, 3, row, 128, peer_b(1))
        d["dn"] = ag_copy(chunk, 4, row, 128, peer_b(3))
        d["s"] = [ag_copy(chunk, 7, row, 128, sibling)]

    def ag_third(chunk):
        d = ag[chunk]
        d["up"].wait_recv()
        below, above = bundle(b_me + 3), bundle(b_me + 1)
        d["f"] = [ag_copy(chunk, 5, below, 64, peer_b(1))]
        d["s"].append(ag_copy(chunk, 8, below, 128, sibling))
        d["dn"].wait_recv()
        d["f"].append(ag_copy(chunk, 6, above + 64, 64, peer_b(3)))
        d["s"].append(ag_copy(chunk, 9, above, 128, sibling))

    def ag_fourth(chunk):
        d = ag[chunk]
        for c in d["f"]:
            c.wait_recv()
        d["s"].append(ag_copy(chunk, 10, bundle(b_me + 2), 128, sibling))

    def ag_last(chunk):
        for c in ag[chunk]["s"]:
            c.wait_recv()

    for chunk in range(3):
        loads[6 + chunk].wait()
        ag_first(chunk)

    scale = 1.0 / HEAD_DIM**0.5
    sub = lax.broadcasted_iota(jnp.int32, (8, 128), 0)
    sub_wide = lax.broadcasted_iota(jnp.int32, (8, 512), 0)
    lane_wide = lax.broadcasted_iota(jnp.int32, (8, 512), 1)
    sub_new = lax.broadcasted_iota(jnp.int32, (8, 16), 0)
    lane_new = lax.broadcasted_iota(jnp.int32, (8, 16), 1)
    contract = (((1,), (1,)), ((), ()))

    def spread(read, base):
        values = jnp.zeros((8, 128), jnp.int32)
        for r in range(8):
            values = jnp.where(sub == r, read(base + r), values)
        return values

    def attend(i):
        kv[2 * i].wait()
        top_rows = pl.ds(16 * i, 16)
        queries = jnp.concatenate([q[top_rows, pl.ds(128 * h, 128)] for h in range(GROUP)], axis=0)
        keys = kk[pl.ds(1024 * i, 1024), :]
        scores = lax.dot_general(queries, keys, contract, preferred_element_type=jnp.float32)
        fresh = lax.dot_general(queries, nk[top_rows, :], contract, preferred_element_type=jnp.float32)
        scores = scores.reshape(8, 2, 8, 1024)
        fresh = fresh.reshape(8, 2, 8, 16)
        kv[2 * i + 1].wait()
        halves = []
        for t in range(2):
            base = 16 * i + 8 * t
            count = spread(lambda r: lens[r], base)[:, :1]
            valid = (lane_wide // CACHE == sub_wide) & (lane_wide % CACHE < count)
            mine = lane_new == sub_new + 8 * t
            s = jnp.where(valid[None], scores[:, t, :, 512 * t : 512 * t + 512] * scale, NEG)
            f = jnp.where(mine[None], fresh[:, t] * scale, NEG)
            top = jnp.maximum(jnp.max(s, axis=2, keepdims=True), jnp.max(f, axis=2, keepdims=True))
            es, ef = jnp.exp(s - top), jnp.exp(f - top)
            total = jnp.sum(es, axis=2, keepdims=True) + jnp.sum(ef, axis=2, keepdims=True)
            inv = 1.0 / total
            ws_ = (es * inv).reshape(64, 512).astype(jnp.bfloat16)
            wf = (ef * inv).reshape(64, 16).astype(jnp.bfloat16)
            o = jnp.dot(ws_, vv[pl.ds(1024 * i + 512 * t, 512), :], preferred_element_type=jnp.float32)
            o = o + jnp.dot(wf, nv[top_rows, :], preferred_element_type=jnp.float32)
            halves.append(o)
        for h in range(GROUP):
            block = jnp.concatenate([o[8 * h : 8 * h + 8] for o in halves], axis=0)
            att[top_rows, pl.ds(128 * h, 128)] = block.astype(jnp.bfloat16)

    def project(n):
        ws[n].wait()
        part[n] = jnp.dot(att[...], w[n], preferred_element_type=jnp.float32)

    rs = {}

    def rs_step(way, step, half):
        n = (0, 1, 3, 5)[step] if way == 0 or step == 0 else (0, 2, 4, 6)[step]
        cols = pl.ds(256 * half, 256)
        value = part[n, :, cols]
        if (way, step - 1, half) in rs:
            rs[way, step - 1, half].wait_recv()
            value = value + rs_dst[way, step - 1, half].astype(jnp.float32)
        rs_src[way, step, half] = value.astype(jnp.bfloat16)
        copy = pltpu.make_async_remote_copy(
            src_ref=rs_src.at[way, step, half], dst_ref=rs_dst.at[way, step, half],
            send_sem=rs_send.at[way, step, half], recv_sem=rs_recv.at[way, step, half],
            device_id=(req, (z + (1 if way == 0 else 7)) % 8), device_id_type=MESH,
        )
        copy.start()
        started.append(copy)
        rs[way, step, half] = copy

    lane_group = lax.broadcasted_iota(jnp.int32, (8, 128), 1) // RANK

    def places(i):
        slot = spread(lambda r: home[ad[r]], 8 * i)
        c, xx, yy = (slot // 2) % 2, (slot // 4) % 4, slot // 16
        place = jnp.where(c == 0, yy * 4 + xx, xx * 4 + yy)
        return (c * 16 + place) * 2 + slot % 2

    for i in (0, 3, 4, 5):
        loads[i].wait()
    attend(0)
    ag_second(0)
    attend(1)
    ag_second(1)
    attend(2)
    ag_second(2)
    attend(3)
    for n in range(0, 1):
        project(n)
    rs_step(0, 0, 0)
    rs_step(1, 0, 1)
    ag_third(0)
    project(1)
    rs_step(0, 1, 1)
    project(2)
    rs_step(1, 1, 0)
    ag_third(1)
    rs_step(0, 1, 0)
    rs_step(1, 1, 1)
    project(3)
    rs_step(0, 2, 1)
    project(4)
    rs_step(1, 2, 0)
    ag_third(2)
    ag_fourth(0)
    rs_step(0, 2, 0)
    rs_step(1, 2, 1)
    project(5)
    project(6)
    rs_step(0, 3, 1)
    rs_step(1, 3, 0)
    rs_step(0, 3, 0)
    rs_step(1, 3, 1)
    ag_fourth(1)
    project(7)

    loads[1].wait()
    loads[2].wait()
    place = [places(i) for i in range(8)]
    ag_last(0)
    inner = lax.dot_general(att[:, pl.ds(0, 512)], gath[0], contract, preferred_element_type=jnp.float32)
    ag_fourth(2)
    ag_last(1)
    inner = inner + lax.dot_general(
        att[:, pl.ds(512, 512)], gath[1], contract, preferred_element_type=jnp.float32
    )
    packed = jnp.zeros((8, 128), jnp.float32)
    for i in range(8):
        one = jnp.zeros((8, 128), jnp.float32)
        for g in range(8):
            hit = lane_group + 8 * g == place[i]
            one = one + jnp.where(hit, inner[8 * i : 8 * i + 8, 128 * g : 128 * g + 128], 0.0)
        for shift in (64, 32, 16):
            one = one + pltpu.roll(one, shift, 1)
        packed = jnp.where(lane_group == i, one, packed)
    low_own[...] = packed
    low_all[z] = packed
    lows = []
    for d in range(1, 8):
        copy = pltpu.make_async_remote_copy(
            src_ref=low_own, dst_ref=low_all.at[z], send_sem=low_send.at[d - 1], recv_sem=low_recv.at[d - 1],
            device_id=(req, (z + d) % 8), device_id_type=MESH,
        )
        copy.start()
        started.append(copy)
        lows.append(copy)
    for copy in lows:
        copy.wait_recv()
    total = low_all[0]
    for j in range(1, 8):
        total = total + low_all[j]
    rows = []
    for i in range(8):
        one = jnp.where(lane_group == i, total, 0.0)
        for shift in (64, 32, 16):
            one = one + pltpu.roll(one, shift, 1)
        rows.append(
            jnp.concatenate([jnp.where(lane_group + 8 * g == place[i], one, 0.0) for g in range(8)], axis=1)
        )
    low = jnp.concatenate(rows, axis=0).astype(jnp.bfloat16)
    ag_last(2)
    delta = jnp.dot(low, gath[2], preferred_element_type=jnp.float32)
    delta = delta.astype(jnp.bfloat16).astype(jnp.float32)
    for half in range(2):
        cols = pl.ds(256 * half, 256)
        value = part[7, :, cols]
        for way in range(2):
            rs[way, 3, half].wait_recv()
            value = value + rs_dst[way, 3, half].astype(jnp.float32)
        value = value + delta[:, 256 * half : 256 * half + 256]
        out_ref[:, cols] = value.astype(jnp.bfloat16)
    for copy in started:
        copy.wait_send()


def per_device(
    queries, key_cache, value_cache, new_key, new_value, cache_length, row_adapter, adapter_home,
    down_pool, up_pool, out_weight,
):
    down = jnp.transpose(down_pool, (0, 2, 1)).reshape(32, 1024)
    up = up_pool.reshape(32, 512)
    keys = key_cache.reshape(4096, 128)
    values = value_cache.reshape(4096, 128)
    named = row_adapter.reshape(64)
    hbm = pl.BlockSpec(memory_space=pltpu.HBM)
    bf16 = jnp.bfloat16
    dma, vmem, smem = pltpu.SemaphoreType.DMA, pltpu.VMEM, pltpu.SMEM
    return pl.pallas_call(
        kernel,
        out_shape=jax.ShapeDtypeStruct((64, 512), bf16),
        in_specs=[hbm] * 11,
        out_specs=pl.BlockSpec(memory_space=pltpu.VMEM),
        scratch_shapes=[
            vmem((64, 1024), bf16),
            vmem((4096, 128), bf16),
            vmem((4096, 128), bf16),
            vmem((64, 128), bf16),
            vmem((64, 128), bf16),
            smem((64,), jnp.int32),
            smem((64,), jnp.int32),
            smem((64,), jnp.int32),
            vmem((3, 1024, 512), bf16),
            vmem((8, 1024, 512), bf16),
            vmem((64, 1024), bf16),
            vmem((8, 64, 512), jnp.float32),
            vmem((8, 128), jnp.float32),
            vmem((8, 8, 128), jnp.float32),
            vmem((2, 4, 2, 64, 256), bf16),
            vmem((2, 4, 2, 64, 256), bf16),
            dma((9,)),
            dma((2, 4)),
            dma((8,)),
            dma((3, 11)),
            dma((3, 11)),
            dma((7,)),
            dma((7,)),
            dma((2, 4, 2)),
            dma((2, 4, 2)),
        ],
        compiler_params=pltpu.CompilerParams(
            collective_id=0, has_side_effects=True, vmem_limit_bytes=60 * 1024 * 1024
        ),
    )(
        queries, keys, values, new_key, new_value, cache_length, named, adapter_home, down, up, out_weight
    )


def solution(mesh):
    return jax.shard_map(
        per_device,
        mesh=mesh,
        in_specs=(
            P("req", "tp"),
            P("req", "tp", None, None),
            P("req", "tp", None, None),
            P("req", "tp"),
            P("req", "tp"),
            P("req"),
            P("req", None),
            P(),
            P("req", "tp", None),
            P("req", None, "tp"),
            P("tp", None),
        ),
        out_specs=P("req", "tp"),
        check_vma=False,
    )
```

time: 125 us -> 38.1 us (0.30)
  waiting for transfers between devices: 75.9 us -> 0 us
  Pallas kernels: 0 us -> 36.5 us
  matrix products: 15.7 us -> 0 us
  between operations: 15 us -> 0.01 us
  blocking collectives: 14 us -> 0 us
  other arithmetic: 3.44 us -> 0 us
    all_gather x2 -> x0, waiting for transfers between devices: 74.4 us -> none  [the longest x1 42.7 us: per_device(): piece = lax.all_gather(down_pool, 'req', axis=0, tiled=True)]
    pallas_call x0 -> x1, Pallas kernels: none -> 36.5 us  [per_device(): pl.pallas_call(kernel, out_shape=jax.ShapeDtypeStruct((64, 512), bf16), i...]
    dot_general x6 -> x0, matrix products: 15.7 us -> none  [the longest x1 5.95 us: per_device(): base = jnp.dot(attended, out_weight, preferred_element_type=jnp.float32)]
    psum x1 -> x0, blocking collectives: 14 us -> none  [per_device(): low = lax.psum(partial_low, 'tp').astype(jnp.bfloat16)]
    convert_element_type x3 -> x0, other arithmetic: 2.28 us -> none  [the longest x1 1.55 us: per_device(): return (share + delta).astype(jnp.bfloat16)]
    unnamed x3 -> x0, waiting for transfers between devices: 1.42 us -> none
  transfers between devices with their start and end apart: 3 -> 0, of which waited for: 2 -> 0; matrix products, arithmetic and copies ran while one was open for 15% -> 0% of each run, Pallas kernels for 0% -> 0%
where the time goes in v1:
time: 38.1 us; the launch traced here: 38 us
  Pallas kernels  36.5 us (96%)
  local copies, waits for them, and re-layouts  1.47 us (4%)
    pallas_call x1, Pallas kernels, per_device(): pl.pallas_call(kernel, out_shape=jax.ShapeDtypeStruct((64, 512), bf16), i...  36.5 us
    unnamed x1, local copies, waits for them, and re-layouts  1.47 us

profile of v1, /device:TPU:1, one launch (start us, length us, event | category | flops | bytes accessed | tf_op | source)
XLA Modules:
  0.0 38.0 jit_solution(1584593435173537879)
XLA Ops:
  0.0 36.5 %shard_map.109 = bf16[64,512]{1,0:T(8,128)(2,1)} custom-call(bf16[64,1024]{1,0:T(8,128)(2,1)} %q_hbm.1, bf16[4096,128]{1,0:T(8,128)(2,1)} %bitcast.7, bf16[4096,128]{1,0:T(8,128)(2,1)} %bitcast.8, bf16[64,128]{1,0:T(8,128)(2,1)} %nk_hbm.1, bf16[64,128]{1,0:T(8,128)(2,1)} %nv_hbm.1, s32[64]{0:T(128)} %len_hbm.1, s32[64]{0:T(128)} %bitcast.11, s32[64]{0:T(128)} %home_hbm.1, ...), custom_call_target="tpu_custom_call" | custom-call | tf_op jit(solution)/shard_map/pallas_call | solution.py:313
  36.5 1.5 %copy.13 = bf16[64,512]{1,0:T(8,128)(2,1)} copy(bf16[64,512]{1,0:T(8,128)(2,1)} %shard_map.109) | data formatting | bytes 131072

commit v2 on v1

v2 whole, which is shorter than its diff:
```python
import jax
import jax.numpy as jnp
from jax import lax
from jax.experimental import pallas as pl
from jax.experimental.pallas import tpu as pltpu
from jax.sharding import PartitionSpec as P

MESH = pl.DeviceIdType.MESH
HEAD_DIM = 128
GROUP = 8
ROWS = 64
CACHE = 64
RANK = 16
NEG = -1e30


def kernel(
    q_hbm, k_hbm, v_hbm, nk_hbm, nv_hbm, len_hbm, ad_hbm, home_hbm, down_hbm, up_hbm, w_hbm,
    out_ref,
    q, kk, vv, nk, nv, lens, ad, home, pool_d, pool_u, w, att, own, rs_src, rs_dst,
    x_src, x_dst, low_own, low_all, y_src, y_dst,
    in_sem, kv_sem, w_sem, pool_send, pool_recv, x_send, x_recv, y_send, y_recv, low_send, low_recv,
    rs_send, rs_recv,
):
    req, z = lax.axis_index("req"), lax.axis_index("tp")
    core = req % 2
    x = (req // 2) % 4
    y = req // 8

    a_me = jnp.where(core == 0, x, y)
    b_me = jnp.where(core == 0, y, x)

    def at(yy, xx, cc):
        return ((yy % 4 * 4 + xx % 4) * 2 + cc, z)

    def peer_a(d):
        return at(y + core * d, x + (1 - core) * d, core)

    def owner(kind, d):
        return at(y + d, x, 0) if kind == 0 else at(y, x + d, 1)

    def source(kind, d):
        return at(y + (1 - core) * d, x + core * d, kind)

    sibling = at(y, x, 1 - core)
    own_bundle = core * 4 + b_me
    sib_bundle = jnp.where(core == 0, 4 + x, y)
    sib_source = (1 - core) * 4 + b_me

    own_rows = pl.ds(pl.multiple_of(a_me * 32, 32), 32)
    loads = [
        (len_hbm, lens), (ad_hbm, ad), (home_hbm, home), (q_hbm, q), (nk_hbm, nk), (nv_hbm, nv),
        (down_hbm, pool_d.at[own_rows]), (up_hbm, pool_u.at[own_rows]),
    ]
    loads = [pltpu.make_async_copy(s, d, in_sem.at[i]) for i, (s, d) in enumerate(loads)]
    for i in (0, 3, 4):
        loads[i].start()
    kv = []
    for i in range(4):
        rows = pl.ds(1024 * i, 1024)
        kv.append(pltpu.make_async_copy(k_hbm.at[rows], kk.at[rows], kv_sem.at[0, i]))
        kv.append(pltpu.make_async_copy(v_hbm.at[rows], vv.at[rows], kv_sem.at[1, i]))
    for c in kv[:2]:
        c.start()
    for i in (5, 6, 7, 1, 2):
        loads[i].start()
    for c in kv[2:]:
        c.start()
    other = [t + (z <= t).astype(jnp.int32) for t in range(7)]
    ws = []
    for t, block in enumerate(other + [z]):
        col = pl.multiple_of(block * 512, 512)
        ws.append(pltpu.make_async_copy(w_hbm.at[:, pl.ds(col, 512)], w.at[t], w_sem.at[t]))
        ws[-1].start()

    barrier = pltpu.get_barrier_semaphore()
    peers = [sibling]
    for d in range(1, 4):
        for c in range(2):
            peers += [at(y + d, x, c), at(y, x + d, c)]
    peers += [(req, (z + d) % 8) for d in range(1, 8)]
    for p in peers:
        pl.semaphore_signal(barrier, inc=1, device_id=p, device_id_type=MESH)

    started = []

    def send(src, dst, send_sem, recv_sem, device):
        copy = pltpu.make_async_remote_copy(
            src_ref=src, dst_ref=dst, send_sem=send_sem, recv_sem=recv_sem, device_id=device, device_id_type=MESH
        )
        copy.start()
        started.append(copy)
        return copy

    def received(src, dst, recv_sem):
        pltpu.make_async_remote_copy(
            src_ref=src, dst_ref=dst, send_sem=low_send.at[0], recv_sem=recv_sem, device_id=sibling,
            device_id_type=MESH,
        ).wait_recv()

    scale = 1.0 / HEAD_DIM**0.5
    sub = lax.broadcasted_iota(jnp.int32, (8, 128), 0)
    sub_wide = lax.broadcasted_iota(jnp.int32, (8, 512), 0)
    lane_wide = lax.broadcasted_iota(jnp.int32, (8, 512), 1)
    sub_new = lax.broadcasted_iota(jnp.int32, (8, 16), 0)
    lane_new = lax.broadcasted_iota(jnp.int32, (8, 16), 1)
    contract = (((1,), (1,)), ((), ()))

    def spread(read, base):
        values = jnp.zeros((8, 128), jnp.int32)
        for r in range(8):
            values = jnp.where(sub == r, read(base + r), values)
        return values

    def attend(i):
        kv[2 * i].wait()
        top_rows = pl.ds(16 * i, 16)
        queries = jnp.concatenate([q[top_rows, pl.ds(128 * h, 128)] for h in range(GROUP)], axis=0)
        keys = kk[pl.ds(1024 * i, 1024), :]
        scores = lax.dot_general(queries, keys, contract, preferred_element_type=jnp.float32)
        fresh = lax.dot_general(queries, nk[top_rows, :], contract, preferred_element_type=jnp.float32)
        scores = scores.reshape(8, 2, 8, 1024)
        fresh = fresh.reshape(8, 2, 8, 16)
        kv[2 * i + 1].wait()
        halves = []
        for t in range(2):
            base = 16 * i + 8 * t
            count = spread(lambda r: lens[r], base)[:, :1]
            valid = (lane_wide // CACHE == sub_wide) & (lane_wide % CACHE < count)
            mine = lane_new == sub_new + 8 * t
            s = jnp.where(valid[None], scores[:, t, :, 512 * t : 512 * t + 512] * scale, NEG)
            f = jnp.where(mine[None], fresh[:, t] * scale, NEG)
            top = jnp.maximum(jnp.max(s, axis=2, keepdims=True), jnp.max(f, axis=2, keepdims=True))
            es, ef = jnp.exp(s - top), jnp.exp(f - top)
            total = jnp.sum(es, axis=2, keepdims=True) + jnp.sum(ef, axis=2, keepdims=True)
            inv = 1.0 / total
            ws_ = (es * inv).reshape(64, 512).astype(jnp.bfloat16)
            wf = (ef * inv).reshape(64, 16).astype(jnp.bfloat16)
            o = jnp.dot(ws_, vv[pl.ds(1024 * i + 512 * t, 512), :], preferred_element_type=jnp.float32)
            o = o + jnp.dot(wf, nv[top_rows, :], preferred_element_type=jnp.float32)
            halves.append(o)
        for h in range(GROUP):
            block = jnp.concatenate([o[8 * h : 8 * h + 8] for o in halves], axis=0)
            att[top_rows, pl.ds(128 * h, 128)] = block.astype(jnp.bfloat16)

    lane = lax.broadcasted_iota(jnp.int32, (8, 128), 1)
    lane_group = lane // RANK

    def place_rows():
        named = [spread(lambda r: ad[r], 8 * i) for i in range(8)]
        slot = jnp.concatenate([spread(lambda r: home[ad[r]], 8 * i) for i in range(8)], axis=0)
        named = jnp.concatenate(named, axis=0)
        row_lane = lax.broadcasted_iota(jnp.int32, (ROWS, 128), 1)
        hot = jnp.where(named == row_lane, 1.0, 0.0).astype(jnp.bfloat16)
        same = lax.dot_general(hot, hot, contract, preferred_element_type=jnp.float32)
        before = lax.broadcasted_iota(jnp.int32, (ROWS, ROWS), 1) < lax.broadcasted_iota(
            jnp.int32, (ROWS, ROWS), 0
        )
        twin = jnp.sum(jnp.where(before, same, 0.0), axis=1, keepdims=True) > 0.5
        c, xx, yy = (slot // 2) % 2, (slot // 4) % 4, slot // 16
        a, b = jnp.where(c == 0, xx, yy), jnp.where(c == 0, yy, xx)
        place = (((c * 4 + b) * 4 + a) * 2 + slot % 2) * 2 + twin.astype(jnp.int32)
        return jnp.where(place == row_lane, 1.0, 0.0).astype(jnp.bfloat16)

    def project(t):
        ws[t].wait()
        value = jnp.dot(att[...], w[t], preferred_element_type=jnp.float32)
        if t == 7:
            own[...] = value
            return
        rs_src[t] = value.astype(jnp.bfloat16)
        send(rs_src.at[t], rs_dst.at[z], rs_send.at[t], rs_recv.at[z], (req, other[t]))

    for i in (0, 3, 4, 5):
        loads[i].wait()
    attend(0)
    attend(1)
    pl.semaphore_wait(barrier, len(peers))

    loads[6].wait()
    loads[7].wait()
    pools = []
    for j, d in enumerate((1, 3, 2)):
        for p, pool in enumerate((pool_d, pool_u)):
            ref = pool.at[own_rows]
            pools.append(send(ref, ref, pool_send.at[p, j], pool_recv.at[p, j], peer_a(d)))
    loads[1].wait()
    loads[2].wait()
    place = place_rows()
    attend(2)
    attend(3)

    moved = lax.dot_general(place, att[...], (((0,), (0,)), ((), ())), preferred_element_type=jnp.float32)
    x_src[...] = moved.astype(jnp.bfloat16).reshape(8, 16, 1024)
    for kind in range(2):
        j = y if kind == 0 else x
        for d in (2, 1, 3):
            send(
                x_src.at[kind * 4 + (j + d) % 4], x_dst.at[core * 4 + j],
                x_send.at[kind * 3 + d - 1], x_recv.at[core * 3 + d - 1], owner(kind, d),
            )
    send(
        x_src.at[sib_bundle], x_dst.at[core * 4 + jnp.where(core == 0, x, y)], x_send.at[6], x_recv.at[6], sibling
    )
    x_dst[own_bundle] = x_src[own_bundle]

    project(0)
    project(1)
    project(2)
    project(3)

    for copy in pools:
        copy.wait_recv()
    for c in range(2):
        for d in range(1, 4):
            here = c * 4 + (b_me - d + 4) % 4
            received(x_src.at[0], x_dst.at[here], x_recv.at[c * 3 + d - 1])
    received(x_src.at[0], x_dst.at[sib_source], x_recv.at[6])

    inner = lax.dot_general(
        x_dst[...].reshape(128, 1024), pool_d[...], contract, preferred_element_type=jnp.float32
    )
    tall = lax.broadcasted_iota(jnp.int32, (128, 128), 0)
    wide_group = lax.broadcasted_iota(jnp.int32, (128, 128), 1) // RANK
    mine = wide_group == (tall % 16) // 2

    def fold(value):
        for shift in (64, 32, 16):
            value = value + pltpu.roll(value, shift, 1)
        return value

    inner = fold(jnp.where(mine, inner, 0.0))
    for half in range(2):
        packed = jnp.zeros((8, 128), jnp.float32)
        for i in range(8):
            row = 64 * half + 8 * i
            packed = jnp.where(lane_group == i, inner[row : row + 8], packed)
        low_own[pl.ds(8 * half, 8), :] = packed
    low_all[z] = low_own[...]
    for d in (4, 3, 5, 2, 6, 1, 7):
        send(low_own, low_all.at[z], low_send.at[d - 1], low_recv.at[d - 1], (req, (z + d) % 8))

    project(4)
    project(5)
    project(6)
    project(7)

    for d in range(1, 8):
        received(low_own, low_all.at[(z - d + 8) % 8], low_recv.at[d - 1])
    total = low_all[0]
    for j in range(1, 8):
        total = total + low_all[j]
    rows = [jnp.where(lane_group == i % 8, total[i // 8 * 8 : i // 8 * 8 + 8], 0.0) for i in range(16)]
    low = jnp.where(mine, fold(jnp.concatenate(rows, axis=0)), 0.0).astype(jnp.bfloat16)
    delta = jnp.dot(low, pool_u[...], preferred_element_type=jnp.float32)
    y_src[...] = delta.astype(jnp.bfloat16).reshape(8, 16, 512)

    for c in range(2):
        for d in (2, 1, 3):
            send(
                y_src.at[c * 4 + (b_me + d) % 4], y_dst.at[own_bundle],
                y_send.at[c * 3 + d - 1], y_recv.at[core * 3 + d - 1], source(c, d),
            )
    send(y_src.at[sib_source], y_dst.at[own_bundle], y_send.at[6], y_recv.at[6], sibling)
    y_dst[own_bundle] = y_src[own_bundle]

    value = own[...]
    for t in range(7):
        received(rs_src.at[t], rs_dst.at[other[t]], rs_recv.at[other[t]])
        value = value + rs_dst[other[t]].astype(jnp.float32)
    own[...] = value

    for kind in range(2):
        j = y if kind == 0 else x
        for d in range(1, 4):
            received(y_src.at[0], y_dst.at[kind * 4 + (j - d + 4) % 4], y_recv.at[kind * 3 + d - 1])
    received(y_src.at[0], y_dst.at[sib_bundle], y_recv.at[6])
    change = jnp.dot(place, y_dst[...].reshape(128, 512), preferred_element_type=jnp.float32)
    out_ref[...] = (own[...] + change).astype(jnp.bfloat16)
    for copy in started:
        copy.wait_send()


def per_device(
    queries, key_cache, value_cache, new_key, new_value, cache_length, row_adapter, adapter_home,
    down_pool, up_pool, out_weight,
):
    down = jnp.transpose(down_pool, (0, 2, 1)).reshape(32, 1024)
    up = up_pool.reshape(32, 512)
    keys = key_cache.reshape(4096, 128)
    values = value_cache.reshape(4096, 128)
    named = row_adapter.reshape(64)
    hbm = pl.BlockSpec(memory_space=pltpu.HBM)
    bf16 = jnp.bfloat16
    dma, vmem, smem = pltpu.SemaphoreType.DMA, pltpu.VMEM, pltpu.SMEM
    return pl.pallas_call(
        kernel,
        out_shape=jax.ShapeDtypeStruct((64, 512), bf16),
        in_specs=[hbm] * 11,
        out_specs=pl.BlockSpec(memory_space=pltpu.VMEM),
        scratch_shapes=[
            vmem((64, 1024), bf16),
            vmem((4096, 128), bf16),
            vmem((4096, 128), bf16),
            vmem((64, 128), bf16),
            vmem((64, 128), bf16),
            smem((64,), jnp.int32),
            smem((64,), jnp.int32),
            smem((64,), jnp.int32),
            vmem((128, 1024), bf16),
            vmem((128, 512), bf16),
            vmem((8, 1024, 512), bf16),
            vmem((64, 1024), bf16),
            vmem((64, 512), jnp.float32),
            vmem((7, 64, 512), bf16),
            vmem((8, 64, 512), bf16),
            vmem((8, 16, 1024), bf16),
            vmem((8, 16, 1024), bf16),
            vmem((16, 128), jnp.float32),
            vmem((8, 16, 128), jnp.float32),
            vmem((8, 16, 512), bf16),
            vmem((8, 16, 512), bf16),
            dma((8,)),
            dma((2, 4)),
            dma((8,)),
            dma((2, 3)),
            dma((2, 3)),
            dma((7,)),
            dma((7,)),
            dma((7,)),
            dma((7,)),
            dma((7,)),
            dma((7,)),
            dma((7,)),
            dma((8,)),
        ],
        compiler_params=pltpu.CompilerParams(
            collective_id=0, has_side_effects=True, vmem_limit_bytes=60 * 1024 * 1024
        ),
    )(
        queries, keys, values, new_key, new_value, cache_length, named, adapter_home, down, up, out_weight
    )


def solution(mesh):
    return jax.shard_map(
        per_device,
        mesh=mesh,
        in_specs=(
            P("req", "tp"),
            P("req", "tp", None, None),
            P("req", "tp", None, None),
            P("req", "tp"),
            P("req", "tp"),
            P("req"),
            P("req", None),
            P(),
            P("req", "tp", None),
            P("req", None, "tp"),
            P("tp", None),
        ),
        out_specs=P("req", "tp"),
        check_vma=False,
    )
```

time: 38.1 us -> 34.4 us (0.903)
  Pallas kernels: 36.5 us -> 32.8 us
    pallas_call x1, Pallas kernels: 36.5 us -> 32.8 us  [per_device(): pl.pallas_call(kernel, out_shape=jax.ShapeDtypeStruct((64, 512), bf16), i...]
where the time goes in v2:
time: 34.4 us; the launch traced here: 34.3 us
  Pallas kernels  32.8 us (95%)
  local copies, waits for them, and re-layouts  1.47 us (4%)
    pallas_call x1, Pallas kernels, per_device(): pl.pallas_call(kernel, out_shape=jax.ShapeDtypeStruct((64, 512), bf16), i...  32.8 us
    unnamed x1, local copies, waits for them, and re-layouts  1.47 us

profile of v2, /device:TPU:1, one launch (start us, length us, event | category | flops | bytes accessed | tf_op | source)
XLA Modules:
  0.0 34.3 jit_solution(1324354345368680128)
XLA Ops:
  0.0 32.8 %shard_map.109 = bf16[64,512]{1,0:T(8,128)(2,1)} custom-call(bf16[64,1024]{1,0:T(8,128)(2,1)} %q_hbm.1, bf16[4096,128]{1,0:T(8,128)(2,1)} %bitcast.7, bf16[4096,128]{1,0:T(8,128)(2,1)} %bitcast.8, bf16[64,128]{1,0:T(8,128)(2,1)} %nk_hbm.1, bf16[64,128]{1,0:T(8,128)(2,1)} %nv_hbm.1, s32[64]{0:T(128)} %len_hbm.1, s32[64]{0:T(128)} %bitcast.11, s32[64]{0:T(128)} %home_hbm.1, ...), custom_call_target="tpu_custom_call" | custom-call | tf_op jit(solution)/shard_map/pallas_call | solution.py:296
  32.8 1.5 %copy.13 = bf16[64,512]{1,0:T(8,128)(2,1)} copy(bf16[64,512]{1,0:T(8,128)(2,1)} %shard_map.109) | data formatting | bytes 131072

commit v3 on v2

--- a/solution.py
+++ b/solution.py
@@ -12,12 +12,13 @@
 CACHE = 64
 RANK = 16
 NEG = -1e30
+ORDER = (4, 3, 5, 1, 7, 2, 6, 0)
 
 
 def kernel(
     q_hbm, k_hbm, v_hbm, nk_hbm, nv_hbm, len_hbm, ad_hbm, home_hbm, down_hbm, up_hbm, w_hbm,
     out_ref,
-    q, kk, vv, nk, nv, lens, ad, home, pool_d, pool_u, w, att, own, rs_src, rs_dst,
+    q, kk, vv, nk, nv, lens, ad, home, pool_d, pool_u, w, att, part, rs_src, rs_dst,
     x_src, x_dst, low_own, low_all, y_src, y_dst,
     in_sem, kv_sem, w_sem, pool_send, pool_recv, x_send, x_recv, y_send, y_recv, low_send, low_recv,
     rs_send, rs_recv,
@@ -66,10 +67,9 @@
         loads[i].start()
     for c in kv[2:]:
         c.start()
-    other = [t + (z <= t).astype(jnp.int32) for t in range(7)]
     ws = []
-    for t, block in enumerate(other + [z]):
-        col = pl.multiple_of(block * 512, 512)
+    for t, o in enumerate(ORDER):
+        col = pl.multiple_of((z + o) % 8 * 512, 512)
         ws.append(pltpu.make_async_copy(w_hbm.at[:, pl.ds(col, 512)], w.at[t], w_sem.at[t]))
         ws[-1].start()
 
@@ -113,7 +113,6 @@
         return values
 
     def attend(i):
-        kv[2 * i].wait()
         top_rows = pl.ds(16 * i, 16)
         queries = jnp.concatenate([q[top_rows, pl.ds(128 * h, 128)] for h in range(GROUP)], axis=0)
         keys = kk[pl.ds(1024 * i, 1024), :]
@@ -121,7 +120,6 @@
         fresh = lax.dot_general(queries, nk[top_rows, :], contract, preferred_element_type=jnp.float32)
         scores = scores.reshape(8, 2, 8, 1024)
         fresh = fresh.reshape(8, 2, 8, 16)
-        kv[2 * i + 1].wait()
         halves = []
         for t in range(2):
             base = 16 * i + 8 * t
@@ -162,33 +160,75 @@
         place = (((c * 4 + b) * 4 + a) * 2 + slot % 2) * 2 + twin.astype(jnp.int32)
         return jnp.where(place == row_lane, 1.0, 0.0).astype(jnp.bfloat16)
 
-    def project(t):
-        ws[t].wait()
-        value = jnp.dot(att[...], w[t], preferred_element_type=jnp.float32)
-        if t == 7:
-            own[...] = value
-            return
-        rs_src[t] = value.astype(jnp.bfloat16)
-        send(rs_src.at[t], rs_dst.at[z], rs_send.at[t], rs_recv.at[z], (req, other[t]))
-
-    for i in (0, 3, 4, 5):
+    def project(first, last):
+        for t in range(first, last):
+            ws[t].wait()
+
+        def step(t, carry):
+            part[t] = jnp.dot(att[...], w[t], preferred_element_type=jnp.float32)
+            return carry
+
+        lax.fori_loop(first, last, step, 0)
+
+    def along(d):
+        return (req, (z + d) % 8)
+
+    def sum_copy(j, way, d):
+        return send(rs_src.at[j, way], rs_dst.at[j, way], rs_send.at[j, way], rs_recv.at[j, way], along(d))
+
+    def first_sums():
+        far = []
+        for way, d in enumerate((2, 6)):
+            cols = pl.ds(256 * way, 256)
+            rs_src[0, way, :, cols] = part[0, :, cols].astype(jnp.bfloat16)
+            far.append(
+                send(
+                    rs_src.at[0, way, :, cols], rs_dst.at[0, way, :, cols], rs_send.at[0, way], rs_recv.at[0, way],
+                    along(d),
+                )
+            )
+        for way, d in enumerate((1, 7)):
+            rs_src[1, way] = part[1 + way].astype(jnp.bfloat16)
+            far.append(sum_copy(1, way, d))
+        near = []
+        for way, d in enumerate((1, 7)):
+            rs_src[2, way] = part[3 + way].astype(jnp.bfloat16)
+            near.append(sum_copy(2, way, d))
+        return far, near
+
+    def second_sums(far):
+        for copy in far:
+            copy.wait_recv()
+        last = []
+        for way, d in enumerate((2, 6)):
+            for half in range(2):
+                cols = pl.ds(256 * half, 256)
+                value = part[5 + way, :, cols] + rs_dst[1, way, :, cols].astype(jnp.float32)
+                if half == way:
+                    value = value + rs_dst[0, way, :, cols].astype(jnp.float32)
+                rs_src[3, way, :, cols] = value.astype(jnp.bfloat16)
+            last.append(sum_copy(3, way, d))
+        return last
+
+    for i in (1, 2):
         loads[i].wait()
-    attend(0)
-    attend(1)
+    place = place_rows()
     pl.semaphore_wait(barrier, len(peers))
 
     loads[6].wait()
     loads[7].wait()
     pools = []
-    for j, d in enumerate((1, 3, 2)):
-        for p, pool in enumerate((pool_d, pool_u)):
+    for p, pool in enumerate((pool_d, pool_u)):
+        for j, d in enumerate((2, 1, 3)):
             ref = pool.at[own_rows]
             pools.append(send(ref, ref, pool_send.at[p, j], pool_recv.at[p, j], peer_a(d)))
-    loads[1].wait()
-    loads[2].wait()
-    place = place_rows()
-    attend(2)
-    attend(3)
+
+    for i in (0, 3, 4, 5):
+        loads[i].wait()
+    for c in kv:
+        c.wait()
+    for i in range(4):
+        attend(i)
 
     moved = lax.dot_general(place, att[...], (((0,), (0,)), ((), ())), preferred_element_type=jnp.float32)
     x_src[...] = moved.astype(jnp.bfloat16).reshape(8, 16, 1024)
@@ -204,12 +244,10 @@
     )
     x_dst[own_bundle] = x_src[own_bundle]
 
-    project(0)
-    project(1)
-    project(2)
-    project(3)
-
-    for copy in pools:
+    project(0, 5)
+    far, near = first_sums()
+
+    for copy in pools[:3]:
         copy.wait_recv()
     for c in range(2):
         for d in range(1, 4):
@@ -240,10 +278,8 @@
     for d in (4, 3, 5, 2, 6, 1, 7):
         send(low_own, low_all.at[z], low_send.at[d - 1], low_recv.at[d - 1], (req, (z + d) % 8))
 
-    project(4)
-    project(5)
-    project(6)
-    project(7)
+    project(5, 8)
+    last = second_sums(far)
 
     for d in range(1, 8):
         received(low_own, low_all.at[(z - d + 8) % 8], low_recv.at[d - 1])
@@ -251,6 +287,8 @@
     for j in range(1, 8):
         total = total + low_all[j]
     rows = [jnp.where(lane_group == i % 8, total[i // 8 * 8 : i // 8 * 8 + 8], 0.0) for i in range(16)]
+    for copy in pools[3:]:
+        copy.wait_recv()
     low = jnp.where(mine, fold(jnp.concatenate(rows, axis=0)), 0.0).astype(jnp.bfloat16)
     delta = jnp.dot(low, pool_u[...], preferred_element_type=jnp.float32)
     y_src[...] = delta.astype(jnp.bfloat16).reshape(8, 16, 512)
@@ -264,11 +302,10 @@
     send(y_src.at[sib_source], y_dst.at[own_bundle], y_send.at[6], y_recv.at[6], sibling)
     y_dst[own_bundle] = y_src[own_bundle]
 
-    value = own[...]
-    for t in range(7):
-        received(rs_src.at[t], rs_dst.at[other[t]], rs_recv.at[other[t]])
-        value = value + rs_dst[other[t]].astype(jnp.float32)
-    own[...] = value
+    for j, copies in ((2, near), (3, last)):
+        for way, copy in enumerate(copies):
+            copy.wait_recv()
+            part[7] = part[7] + rs_dst[j, way].astype(jnp.float32)
 
     for kind in range(2):
         j = y if kind == 0 else x
@@ -276,7 +313,7 @@
             received(y_src.at[0], y_dst.at[kind * 4 + (j - d + 4) % 4], y_recv.at[kind * 3 + d - 1])
     received(y_src.at[0], y_dst.at[sib_bundle], y_recv.at[6])
     change = jnp.dot(place, y_dst[...].reshape(128, 512), preferred_element_type=jnp.float32)
-    out_ref[...] = (own[...] + change).astype(jnp.bfloat16)
+    out_ref[...] = (part[7] + change).astype(jnp.bfloat16)
     for copy in started:
         copy.wait_send()
 
@@ -311,9 +348,9 @@
             vmem((128, 512), bf16),
             vmem((8, 1024, 512), bf16),
             vmem((64, 1024), bf16),
-            vmem((64, 512), jnp.float32),
-            vmem((7, 64, 512), bf16),
-            vmem((8, 64, 512), bf16),
+            vmem((8, 64, 512), jnp.float32),
+            vmem((4, 2, 64, 512), bf16),
+            vmem((4, 2, 64, 512), bf16),
             vmem((8, 16, 1024), bf16),
             vmem((8, 16, 1024), bf16),
             vmem((16, 128), jnp.float32),
@@ -331,8 +368,8 @@
             dma((7,)),
             dma((7,)),
             dma((7,)),
-            dma((7,)),
-            dma((8,)),
+            dma((4, 2)),
+            dma((4, 2)),
         ],
         compiler_params=pltpu.CompilerParams(
             collective_id=0, has_side_effects=True, vmem_limit_bytes=60 * 1024 * 1024

time: 34.4 us -> 29.8 us (0.87)
  Pallas kernels: 32.8 us -> 28.1 us
    pallas_call x1, Pallas kernels: 32.8 us -> 28.1 us  [per_device(): pl.pallas_call(kernel, out_shape=jax.ShapeDtypeStruct((64, 512), bf16), i...]
where the time goes in v3:
time: 29.8 us; the launch traced here: 29.5 us
  Pallas kernels  28.1 us (94%)
  local copies, waits for them, and re-layouts  1.47 us (5%)
    pallas_call x1, Pallas kernels, per_device(): pl.pallas_call(kernel, out_shape=jax.ShapeDtypeStruct((64, 512), bf16), i...  28.1 us
    unnamed x1, local copies, waits for them, and re-layouts  1.47 us

profile of v3, /device:TPU:1, one launch (start us, length us, event | category | flops | bytes accessed | tf_op | source)
XLA Modules:
  0.0 29.5 jit_solution(15093521913214375561)
XLA Ops:
  0.0 28.1 %shard_map.109 = bf16[64,512]{1,0:T(8,128)(2,1)} custom-call(bf16[64,1024]{1,0:T(8,128)(2,1)} %q_hbm.1, bf16[4096,128]{1,0:T(8,128)(2,1)} %bitcast.7, bf16[4096,128]{1,0:T(8,128)(2,1)} %bitcast.8, bf16[64,128]{1,0:T(8,128)(2,1)} %nk_hbm.1, bf16[64,128]{1,0:T(8,128)(2,1)} %nv_hbm.1, s32[64]{0:T(128)} %len_hbm.1, s32[64]{0:T(128)} %bitcast.11, s32[64]{0:T(128)} %home_hbm.1, ...), custom_call_target="tpu_custom_call" | custom-call | tf_op jit(solution)/shard_map/pallas_call | solution.py:333
  28.1 1.5 %copy.13 = bf16[64,512]{1,0:T(8,128)(2,1)} copy(bf16[64,512]{1,0:T(8,128)(2,1)} %shard_map.109) | data formatting | bytes 131072

commit v4 on v3

--- a/solution.py
+++ b/solution.py
@@ -71,7 +71,6 @@
     for t, o in enumerate(ORDER):
         col = pl.multiple_of((z + o) % 8 * 512, 512)
         ws.append(pltpu.make_async_copy(w_hbm.at[:, pl.ds(col, 512)], w.at[t], w_sem.at[t]))
-        ws[-1].start()
 
     barrier = pltpu.get_barrier_semaphore()
     peers = [sibling]
@@ -190,11 +189,14 @@
         for way, d in enumerate((1, 7)):
             rs_src[1, way] = part[1 + way].astype(jnp.bfloat16)
             far.append(sum_copy(1, way, d))
+        return far
+
+    def near_sums():
         near = []
         for way, d in enumerate((1, 7)):
             rs_src[2, way] = part[3 + way].astype(jnp.bfloat16)
             near.append(sum_copy(2, way, d))
-        return far, near
+        return near
 
     def second_sums(far):
         for copy in far:
@@ -210,9 +212,12 @@
             last.append(sum_copy(3, way, d))
         return last
 
-    for i in (1, 2):
+    for i in (0, 3, 4, 5):
         loads[i].wait()
-    place = place_rows()
+    for c in kv[:4]:
+        c.wait()
+    attend(0)
+    attend(1)
     pl.semaphore_wait(barrier, len(peers))
 
     loads[6].wait()
@@ -222,13 +227,16 @@
         for j, d in enumerate((2, 1, 3)):
             ref = pool.at[own_rows]
             pools.append(send(ref, ref, pool_send.at[p, j], pool_recv.at[p, j], peer_a(d)))
-
-    for i in (0, 3, 4, 5):
+    for c in ws:
+        c.start()
+
+    for i in (1, 2):
         loads[i].wait()
-    for c in kv:
+    for c in kv[4:]:
         c.wait()
-    for i in range(4):
-        attend(i)
+    place = place_rows()
+    attend(2)
+    attend(3)
 
     moved = lax.dot_general(place, att[...], (((0,), (0,)), ((), ())), preferred_element_type=jnp.float32)
     x_src[...] = moved.astype(jnp.bfloat16).reshape(8, 16, 1024)
@@ -245,7 +253,7 @@
     x_dst[own_bundle] = x_src[own_bundle]
 
     project(0, 5)
-    far, near = first_sums()
+    far = first_sums()
 
     for copy in pools[:3]:
         copy.wait_recv()
@@ -268,24 +276,27 @@
         return value
 
     inner = fold(jnp.where(mine, inner, 0.0))
+    halves = []
     for half in range(2):
         packed = jnp.zeros((8, 128), jnp.float32)
         for i in range(8):
             row = 64 * half + 8 * i
             packed = jnp.where(lane_group == i, inner[row : row + 8], packed)
-        low_own[pl.ds(8 * half, 8), :] = packed
+        halves.append(packed)
+    low_own[...] = jnp.concatenate(halves, axis=0).astype(jnp.bfloat16)
     low_all[z] = low_own[...]
     for d in (4, 3, 5, 2, 6, 1, 7):
         send(low_own, low_all.at[z], low_send.at[d - 1], low_recv.at[d - 1], (req, (z + d) % 8))
 
+    near = near_sums()
     project(5, 8)
     last = second_sums(far)
 
     for d in range(1, 8):
         received(low_own, low_all.at[(z - d + 8) % 8], low_recv.at[d - 1])
-    total = low_all[0]
+    total = low_all[0].astype(jnp.float32)
     for j in range(1, 8):
-        total = total + low_all[j]
+        total = total + low_all[j].astype(jnp.float32)
     rows = [jnp.where(lane_group == i % 8, total[i // 8 * 8 : i // 8 * 8 + 8], 0.0) for i in range(16)]
     for copy in pools[3:]:
         copy.wait_recv()
@@ -353,8 +364,8 @@
             vmem((4, 2, 64, 512), bf16),
             vmem((8, 16, 1024), bf16),
             vmem((8, 16, 1024), bf16),
-            vmem((16, 128), jnp.float32),
-            vmem((8, 16, 128), jnp.float32),
+            vmem((16, 128), bf16),
+            vmem((8, 16, 128), bf16),
             vmem((8, 16, 512), bf16),
             vmem((8, 16, 512), bf16),
             dma((8,)),

time: 29.8 us -> 28 us (0.940)
  Pallas kernels: 28.1 us -> 26.4 us
    pallas_call x1, Pallas kernels: 28.1 us -> 26.4 us  [per_device(): pl.pallas_call(kernel, out_shape=jax.ShapeDtypeStruct((64, 512), bf16), i...]
where the time goes in v4:
time: 28 us; the launch traced here: 27.9 us
  Pallas kernels  26.4 us (94%)
  local copies, waits for them, and re-layouts  1.47 us (5%)
    pallas_call x1, Pallas kernels, per_device(): pl.pallas_call(kernel, out_shape=jax.ShapeDtypeStruct((64, 512), bf16), i...  26.4 us
    unnamed x1, local copies, waits for them, and re-layouts  1.47 us

profile of v4, /device:TPU:1, one launch (start us, length us, event | category | flops | bytes accessed | tf_op | source)
XLA Modules:
  0.0 27.9 jit_solution(15027024610074024672)
XLA Ops:
  0.0 26.4 %shard_map.109 = bf16[64,512]{1,0:T(8,128)(2,1)} custom-call(bf16[64,1024]{1,0:T(8,128)(2,1)} %q_hbm.1, bf16[4096,128]{1,0:T(8,128)(2,1)} %bitcast.7, bf16[4096,128]{1,0:T(8,128)(2,1)} %bitcast.8, bf16[64,128]{1,0:T(8,128)(2,1)} %nk_hbm.1, bf16[64,128]{1,0:T(8,128)(2,1)} %nv_hbm.1, s32[64]{0:T(128)} %len_hbm.1, s32[64]{0:T(128)} %bitcast.11, s32[64]{0:T(128)} %home_hbm.1, ...), custom_call_target="tpu_custom_call" | custom-call | tf_op jit(solution)/shard_map/pallas_call | solution.py:344
  26.4 1.5 %copy.13 = bf16[64,512]{1,0:T(8,128)(2,1)} copy(bf16[64,512]{1,0:T(8,128)(2,1)} %shard_map.109) | data formatting | bytes 131072

commit v5 on v4

--- a/solution.py
+++ b/solution.py
@@ -47,6 +47,14 @@
     own_bundle = core * 4 + b_me
     sib_bundle = jnp.where(core == 0, 4 + x, y)
     sib_source = (1 - core) * 4 + b_me
+
+    barrier = pltpu.get_barrier_semaphore()
+    peers = [(req, (z + d) % 8) for d in (4, 3, 5, 2, 6, 1, 7)] + [sibling]
+    for d in (2, 1, 3):
+        for c in range(2):
+            peers += [at(y + d, x, c), at(y, x + d, c)]
+    for p in peers:
+        pl.semaphore_signal(barrier, inc=1, device_id=p, device_id_type=MESH)
 
     own_rows = pl.ds(pl.multiple_of(a_me * 32, 32), 32)
     loads = [
@@ -71,15 +79,6 @@
     for t, o in enumerate(ORDER):
         col = pl.multiple_of((z + o) % 8 * 512, 512)
         ws.append(pltpu.make_async_copy(w_hbm.at[:, pl.ds(col, 512)], w.at[t], w_sem.at[t]))
-
-    barrier = pltpu.get_barrier_semaphore()
-    peers = [sibling]
-    for d in range(1, 4):
-        for c in range(2):
-            peers += [at(y + d, x, c), at(y, x + d, c)]
-    peers += [(req, (z + d) % 8) for d in range(1, 8)]
-    for p in peers:
-        pl.semaphore_signal(barrier, inc=1, device_id=p, device_id_type=MESH)
 
     started = []
 
@@ -304,6 +303,7 @@
     delta = jnp.dot(low, pool_u[...], preferred_element_type=jnp.float32)
     y_src[...] = delta.astype(jnp.bfloat16).reshape(8, 16, 512)
 
+    earlier = len(started)
     for c in range(2):
         for d in (2, 1, 3):
             send(
@@ -317,6 +317,8 @@
         for way, copy in enumerate(copies):
             copy.wait_recv()
             part[7] = part[7] + rs_dst[j, way].astype(jnp.float32)
+    for copy in started[:earlier]:
+        copy.wait_send()
 
     for kind in range(2):
         j = y if kind == 0 else x
@@ -325,7 +327,7 @@
     received(y_src.at[0], y_dst.at[sib_bundle], y_recv.at[6])
     change = jnp.dot(place, y_dst[...].reshape(128, 512), preferred_element_type=jnp.float32)
     out_ref[...] = (part[7] + change).astype(jnp.bfloat16)
-    for copy in started:
+    for copy in started[earlier:]:
         copy.wait_send()
 
 

time: 28 us -> 28 us (level)
  no operation moved by 1% of the time
where the time goes in v5:
time: 28 us; the launch traced here: 27.8 us
  Pallas kernels  26.3 us (94%)
  local copies, waits for them, and re-layouts  1.47 us (5%)
    pallas_call x1, Pallas kernels, per_device(): pl.pallas_call(kernel, out_shape=jax.ShapeDtypeStruct((64, 512), bf16), i...  26.3 us
    unnamed x1, local copies, waits for them, and re-layouts  1.47 us

profile of v5, /device:TPU:1, one launch (start us, length us, event | category | flops | bytes accessed | tf_op | source)
XLA Modules:
  0.0 27.8 jit_solution(5242484354450271388)
XLA Ops:
  0.0 26.3 %shard_map.109 = bf16[64,512]{1,0:T(8,128)(2,1)} custom-call(bf16[64,1024]{1,0:T(8,128)(2,1)} %q_hbm.1, bf16[4096,128]{1,0:T(8,128)(2,1)} %bitcast.7, bf16[4096,128]{1,0:T(8,128)(2,1)} %bitcast.8, bf16[64,128]{1,0:T(8,128)(2,1)} %nk_hbm.1, bf16[64,128]{1,0:T(8,128)(2,1)} %nv_hbm.1, s32[64]{0:T(128)} %len_hbm.1, s32[64]{0:T(128)} %bitcast.11, s32[64]{0:T(128)} %home_hbm.1, ...), custom_call_target="tpu_custom_call" | custom-call | tf_op jit(solution)/shard_map/pallas_call | solution.py:346
  26.4 1.5 %copy.13 = bf16[64,512]{1,0:T(8,128)(2,1)} copy(bf16[64,512]{1,0:T(8,128)(2,1)} %shard_map.109) | data formatting | bytes 131072
